TPU v7x, 512 devices: a whole 4x4x16 slice. The times are simulated.
512 devices in a mesh: orb: 8 (over y, x_lo), grid: 64 (over x_hi, z, core).
Axes of the slice: x: 4 (x_hi: 2, x_lo: 2; x = x_hi * 2 + x_lo), y: 4, z: 16, core: 2. Of those that a mesh axis runs over, the one named last changes fastest.
Arguments:
- random_orbitals: float32 [8, 256, 256, 256], P('orb', 'grid'), may hold values from -6 to 6
- potential: float32 [256, 256, 256], P('grid'), may hold values from -1.5 to 0.5
- sphere_cells: int32 [1024, 2, 128], P('grid'), may hold values from 0 to 65535, as said below
- projectors: float32 [1024, 4, 128], P('grid'), may hold values from -0.9 to 0.9
- kb_energy: float32 [4], replicated, may hold values from 0.5 to 1.5
- cheb_coef: float32 [3], replicated, may hold values from 0.5 to 1.5
Outputs:
- density: float32 [256, 256, 256], P('grid')
Inputs may be any that keep to these rules, and one draw needn't show every extreme that they name: `sphere_cells`: for each atom a the 128 points are distinct cells: the 128 offsets (dz, dy, dx) with |dz|, |dy|, |dx| <= 3 nearest to the atom's centre, ties broken by the order of (dz, dy, dx) from smallest to largest, added to the centre with periodic wrap along each dimension; row 0 holds the z-plane and row 1 the cell y * 256 + x. The centre's z lies in the slab of planes (a // 16) * 4 to (a // 16) * 4 + 3. Spheres of different atoms may share cells.
All inputs are finite; a program needn't handle non-finite values.
Results may differ from a plain program's by a relative error of at most 0.0002.
Values sent between devices are 32-bit elements; how exact they have to be, the bound alone decides.
A program may use at most 64 MiB of HBM per device.

v0:
```python
import math
import jax
import jax.numpy as jnp
from jax import lax
from jax.sharding import PartitionSpec as P

REACH = 3
PRECISE = lax.Precision.HIGHEST
CENTRE = 2.0
HALF_RANGE = 4.0


def with_halo(cells, sides, width):
    for axis, dim in sides:
        count = lax.axis_size(axis)
        head = lax.slice_in_dim(cells, 0, width, axis=dim)
        tail = lax.slice_in_dim(cells, cells.shape[dim] - width, cells.shape[dim], axis=dim)
        cells = jnp.concatenate(
            [
                lax.ppermute(tail, axis, [(i, (i + 1) % count) for i in range(count)]),
                cells,
                lax.ppermute(head, axis, [((i + 1) % count, i) for i in range(count)]),
            ],
            axis=dim,
        )
    return cells


def from_behind(block, axis, distance):
    devices = range(lax.axis_size(axis))
    route = [((i - distance) % len(devices), i) for i in devices]
    return lax.ppermute(block, axis, route)


def kinetic_table(length):
    places = jnp.arange(length)
    offset = places[:, None] - places[None, :]
    parity = jnp.where(offset % 2 == 0, 1.0, -1.0).astype(jnp.float32)
    angle_half = offset.astype(jnp.float32) * (math.pi / length)
    sine = jnp.where(offset == 0, 1.0, jnp.sin(angle_half))
    off_diag = parity / (2.0 * sine * sine)
    on_diag = jnp.float32(length * length / 12.0 + 1.0 / 6.0)
    return jnp.where(offset == 0, on_diag, off_diag) * (4.0 / (length * length))


def local(random_orbitals, potential, sphere_cells, projectors, kb_energy, cheb_coef):
    grid_count = lax.axis_size("grid")
    grid_pos = lax.axis_index("grid")
    planes = potential.shape[0]
    rows_y = potential.shape[1]
    cols_x = potential.shape[2]
    all_planes = planes * grid_count
    plane_cells = rows_y * cols_x
    first_plane = grid_pos * planes
    orb_count = random_orbitals.shape[0]
    per_dev = sphere_cells.shape[0]
    kinetic_x = kinetic_table(cols_x)
    kinetic_y = kinetic_table(rows_y)
    kinetic_z = kinetic_table(all_planes)

    def along_z(columns):
        turned = jnp.einsum("ozyx,zw->owyx", columns, kinetic_z, precision=PRECISE)
        return lax.all_to_all(turned, "grid", split_axis=1, concat_axis=2, tiled=True)

    z_glob = sphere_cells[:, 0, :]
    in_plane = sphere_cells[:, 1, :]
    local_plane = (z_glob - first_plane + REACH) % all_planes
    ghost_index = (local_plane * plane_cells + in_plane).reshape(-1)

    def nonlocal_term(vector):
        extended = with_halo(vector, (("grid", 1),), REACH)
        flattened = extended.reshape(orb_count, -1)
        values = flattened[:, ghost_index].reshape(orb_count, per_dev, -1)
        coeffs = jnp.einsum("oaj,apj->oap", values, projectors, precision=PRECISE) * kb_energy
        spread = jnp.einsum("oap,apj->oaj", coeffs, projectors, precision=PRECISE).reshape(
            orb_count, -1
        )
        placed = jnp.zeros_like(flattened).at[:, ghost_index].add(spread).reshape(extended.shape)
        lower_rim = placed[:, :REACH]
        upper_rim = placed[:, REACH + planes :]
        from_above = from_behind(lower_rim, "grid", -1)
        from_below = from_behind(upper_rim, "grid", 1)
        interior = placed[:, REACH : REACH + planes]
        interior = interior.at[:, :REACH].add(from_below)
        interior = interior.at[:, planes - REACH :].add(from_above)
        return interior

    def apply_hamiltonian(vector):
        kinetic = jnp.dot(vector.reshape(-1, cols_x), kinetic_x, precision=PRECISE).reshape(
            vector.shape
        )
        kinetic = kinetic + jnp.einsum("ozyx,yw->ozwx", vector, kinetic_y, precision=PRECISE)
        kinetic = kinetic + along_z(
            lax.all_to_all(vector, "grid", split_axis=2, concat_axis=1, tiled=True)
        )
        summed = kinetic + potential * vector + nonlocal_term(vector)
        return (summed - CENTRE * vector) / HALF_RANGE

    first_term = apply_hamiltonian(random_orbitals)
    second_term = 2.0 * apply_hamiltonian(first_term) - random_orbitals
    filtered = (
        cheb_coef[0] * random_orbitals + cheb_coef[1] * first_term + cheb_coef[2] * second_term
    )
    group_density = jnp.sum(filtered * filtered, axis=0)
    density = lax.psum(group_density, "orb")
    return density / (orb_count * lax.axis_size("orb"))


def solution(mesh):
    in_specs = (
        P("orb", "grid", None, None),
        P("grid", None, None),
        P("grid", None, None),
        P("grid", None, None),
        P(),
        P(),
    )
    out_specs = P("grid", None, None)
    return jax.shard_map(local, mesh=mesh, in_specs=in_specs, out_specs=out_specs, check_vma=False)
```

profile of v0, /device:TPU:4, one launch (start us, length us, event | category | flops | bytes accessed | tf_op | source)
XLA Modules:
  0.0 507.4 jit_solution(14557212406994386126)
XLA Ops:
  6.5 1.9 copy.20
  8.4 70.6 %all_to_all.66 = f32[1,4,256,256]{3,1,0,2:T(4,128)S(1)} all-to-all(f32[1,4,256,256]{3,1,0,2:T(4,128)S(1)} %copy.20), channel_id=1, replica_groups=mesh['orb'=8,'grid'=64] {'grid'}, dimensions={2} | all-to-all | bytes 2097152 | tf_op jit(solution)/shard_map/all_to_all | solution.py:94
  79.6 2.1 convolution_bitcast_fusion.3
  81.7 1.6 copy.22
  83.3 9.8 %all-to-all-start.1 = ((f32[1,256,4,256]{3,2,0,1:T(4,128)}), f32[1,256,4,256]{3,2,0,1:T(4,128)}, u32[]{:S(2)}, u32[]{:S(2)}) async-start(f32[1,256,4,256]{3,2,0,1:T(4,128)} %copy.22), calls=%async_computation.1 | async-start | bytes 2097152 | tf_op jit(solution)/shard_map/all_to_all | solution.py:63
  93.1 1.0 fusion.111
  94.1 2.0 collective-permute-start
  96.2 7.1 %collective-permute-start.1 = (f32[1,3,256,256]{3,2,1,0:T(8,128)S(1)}, f32[1,3,256,256]{3,2,1,0:T(8,128)S(1)}, u32[]{:S(2)}, u32[]{:S(2)}) collective-permute-start(f32[1,3,256,256]{3,2,1,0:T(8,128)S(1)} %get-tuple-element.60), channel_id=1, source_target_pairs={{1,0},{2,1},{3,2},{4,3},{5,4},{6,5},{7,6},{8,7},{9,8},{10,9},{11,1... | collective-permute-start | bytes 2359304 | tf_op jit(solution)/shard_map/ppermute | solution.py:22
  103.4 46.4 %collective-permute-done = f32[1,3,256,256]{3,2,1,0:T(8,128)S(1)} collective-permute-done((f32[1,3,256,256]{3,2,1,0:T(8,128)}, f32[1,3,256,256]{3,2,1,0:T(8,128)S(1)}, u32[]{:S(2)}, u32[]{:S(2)}) %collective-permute-start) | collective-permute-done | bytes 786464 | tf_op jit(solution)/shard_map/ppermute | solution.py:20
  150.0 1.3 copy.40
  151.3 11.8 %gather_fusion = f32[2048]{0:T(1024)S(1)} fusion(f32[655360]{0:T(1024)S(1)} %bitcast.161, s32[2048]{0:T(1024)S(1)} %broadcast_clamp_fusion), kind=kCustom, calls=%fused_computation | custom fusion | bytes 24576 | tf_op jit(solution)/shard_map/gather | solution.py:73
  163.7 11.9 %scatter_custom_fusion = f32[655360]{0:T(1024)S(1)} fusion(s32[2048]{0:T(1024)S(1)} %bitcast.173, f32[2048]{0:T(1024)S(1)} %bitcast.182, f32[]{:T(128)} %constant.158.clone.1), kind=kCustom, calls=%fused_computation.14 | custom fusion | flops 2048 | bytes 2621444 | tf_op jit(solution)/shard_map/scatter-add | solution.py:78
  175.6 1.9 reshape.291
  177.5 2.8 fusion.109
  180.3 1.9 collective-permute-start.2
  182.2 7.4 %collective-permute-start.3 = (f32[1,3,256,256]{3,2,1,0:T(8,128)}, f32[1,3,256,256]{3,2,1,0:T(8,128)}, u32[]{:S(2)}, u32[]{:S(2)}) collective-permute-start(f32[1,3,256,256]{3,2,1,0:T(8,128)} %get-tuple-element.55), channel_id=1, source_target_pairs={{1,0},{2,1},{3,2},{4,3},{5,4},{6,5},{7,6},{8,7},{9,8},{10,9},{11,1... | collective-permute-start | bytes 2359304 | tf_op jit(solution)/shard_map/ppermute | solution.py:32
  189.7 2.1 convolution_bitcast_fusion.5
  191.8 1.3 copy.38
  193.1 4.4 collective-permute-done.2
  197.6 1.5 fusion.26
  199.3 1.3 fusion.25
  200.6 1.4 copy.48
  202.0 1.3 all_to_all.54
  203.4 5.2 %broadcast_multiply_fusion.1 = (f32[1,4,256,256]{3,2,1,0:T(8,128)S(1)}, f32[1,4,256,256]{3,2,1,0:T(8,128)}) fusion(f32[1,4,256,256]{3,2,1,0:T(8,128)S(1)} %copy-done.2, f32[1,4,256,256]{3,2,1,0:T(8,128)S(1)} %fusion.25, f32[4,256,256]{2,1,0:T(8,128)} %param.15, f32[1,4,256,256]{3,2,1,0:T(8,128)} %all_to_all.54, f32[1,4,256,256]{3,2,1,0:T(8,128)} %bitcast.165), kind=kOutput, calls=%fused_computation.50 | convolution fusion | flops 808910848 | bytes 7340032 | tf_op jit(solution)/shard_map/ozyx,yw->ozwx/dot_general | solution.py:92
  209.2 63.0 %all_to_all.67 = f32[1,4,256,256]{3,1,0,2:T(4,128)S(1)} all-to-all(f32[1,4,256,256]{3,1,0,2:T(4,128)S(1)} %copy.25), channel_id=1, replica_groups=mesh['orb'=8,'grid'=64] {'grid'}, dimensions={2} | all-to-all | bytes 2097152 | tf_op jit(solution)/shard_map/all_to_all | solution.py:94
  272.8 2.1 convolution_bitcast_fusion
  274.9 1.7 copy.27
  276.6 9.6 %all-to-all-start.3 = ((f32[1,256,4,256]{3,2,0,1:T(4,128)}), f32[1,256,4,256]{3,2,0,1:T(4,128)}, u32[]{:S(2)}, u32[]{:S(2)}) async-start(f32[1,256,4,256]{3,2,0,1:T(4,128)} %copy.27), calls=%async_computation.3 | async-start | bytes 2097152 | tf_op jit(solution)/shard_map/all_to_all | solution.py:63
  286.4 2.1 collective-permute-start.4
  288.4 7.3 %collective-permute-start.5 = (f32[1,3,256,256]{3,2,1,0:T(8,128)S(1)}, f32[1,3,256,256]{3,2,1,0:T(8,128)S(1)}, u32[]{:S(2)}, u32[]{:S(2)}) collective-permute-start(f32[1,3,256,256]{3,2,1,0:T(8,128)S(1)} %get-tuple-element.58), channel_id=1, source_target_pairs={{1,0},{2,1},{3,2},{4,3},{5,4},{6,5},{7,6},{8,7},{9,8},{10,9},{11,1... | collective-permute-start | bytes 2359304 | tf_op jit(solution)/shard_map/ppermute | solution.py:22
  295.8 47.1 %collective-permute-done.4 = f32[1,3,256,256]{3,2,1,0:T(8,128)S(1)} collective-permute-done((f32[1,3,256,256]{3,2,1,0:T(8,128)S(1)}, f32[1,3,256,256]{3,2,1,0:T(8,128)S(1)}, u32[]{:S(2)}, u32[]{:S(2)}) %collective-permute-start.4) | collective-permute-done | bytes 786464 | tf_op jit(solution)/shard_map/ppermute | solution.py:20
  343.1 1.3 copy.41
  344.5 11.8 %gather_fusion.1 = f32[2048]{0:T(1024)S(1)} fusion(f32[655360]{0:T(1024)S(1)} %bitcast.160, s32[2048]{0:T(1024)S(1)} %broadcast_clamp_fusion), kind=kCustom, calls=%fused_computation.1 | custom fusion | bytes 24576 | tf_op jit(solution)/shard_map/gather | solution.py:73
  356.8 12.9 %scatter_custom_fusion.1 = f32[655360]{0:T(1024)} fusion(s32[2048]{0:T(1024)S(1)} %bitcast.174, f32[2048]{0:T(1024)S(1)} %bitcast.181, f32[]{:T(128)} %constant.158.clone.1), kind=kCustom, calls=%fused_computation.12 | custom fusion | flops 2048 | bytes 2621444 | tf_op jit(solution)/shard_map/scatter-add | solution.py:78
  369.7 2.7 reshape.296
  372.7 2.1 collective-permute-start.6
  374.7 7.3 %collective-permute-start.7 = (f32[1,3,256,256]{3,2,1,0:T(8,128)S(1)}, f32[1,3,256,256]{3,2,1,0:T(8,128)S(1)}, u32[]{:S(2)}, u32[]{:S(2)}) collective-permute-start(f32[1,3,256,256]{3,2,1,0:T(8,128)S(1)} %get-tuple-element.53), channel_id=1, source_target_pairs={{1,0},{2,1},{3,2},{4,3},{5,4},{6,5},{7,6},{8,7},{9,8},{10,9},{11,1... | collective-permute-start | bytes 2359304 | tf_op jit(solution)/shard_map/ppermute | solution.py:32
  383.3 3.1 convolution_bitcast_fusion.1
  386.4 1.1 slice.193
  387.4 2.3 collective-permute-done.6
  389.7 1.0 fusion.24
  390.7 0.7 collective-permute-done.7
  391.5 2.2 fusion.23
  393.7 2.5 copy.46
  396.2 2.6 all_to_all.61
  398.8 6.6 %fusion.21 = f32[4,256,256]{2,1,0:T(8,128)} fusion(f32[1,4,256,256]{3,2,1,0:T(8,128)S(1)} %copy-done.3, f32[1,4,256,256]{3,2,1,0:T(8,128)} %fusion.23, f32[4,256,256]{2,1,0:T(8,128)S(1)} %copy-done.4, f32[1,4,256,256]{3,2,1,0:T(8,128)S(1)} %copy-done.6, f32[]{:T(128)} %bitcast.28, f32[]{:T(128)} %bitcast.27, f32[]{:T(128)} %bitcast, ...), kind=kOutput, calls=%fused_computation.35 | convolution fusion | flops 811270144 | bytes 7340044 | tf_op jit(solution)/shard_map/dot_general | solution.py:89
  405.3 92.9 %all-reduce.2.cloned.1.call-done = f32[4,256,256]{2,1,0:T(8,128)} async-done(((f32[4,256,256]{2,1,0:T(8,128)}), f32[4,256,256]{2,1,0:T(8,128)}) %all-reduce.2.cloned.1.call-update) | async-done | bytes 1048592 | tf_op jit(solution)/shard_map/psum | solution.py:105
  498.2 2.3 broadcast_multiply_fusion
  (47 shorter events, 4.6 us)
Async XLA Ops:
  6.5 156.6 %copy-start = (f32[16,4,128]{2,1,0:T(4,128)S(1)}, f32[16,4,128]{2,1,0:T(4,128)}, u32[]{:S(2)}) copy-start(f32[16,4,128]{2,1,0:T(4,128)} %param.17) | copy-start | bytes 98308
  81.6 11.4 %copy-start.1 = (f32[1,4,256,256]{3,2,1,0:T(8,128)S(1)}, f32[1,4,256,256]{3,2,1,0:T(8,128)}, u32[]{:S(2)}) copy-start(f32[1,4,256,256]{3,2,1,0:T(8,128)} %param.14) | copy-start | bytes 3145732
  83.3 20.0 %copy-start.7 = (s32[16,2,128]{2,1,0:T(2,128)S(1)}, s32[16,2,128]{2,1,0:T(2,128)}, u32[]{:S(2)}) copy-start(s32[16,2,128]{2,1,0:T(2,128)} %param.16) | copy-start | bytes 49156
  83.3 117.3 %all-to-all-start.1 = ((f32[1,256,4,256]{3,2,0,1:T(4,128)}), f32[1,256,4,256]{3,2,0,1:T(4,128)}, u32[]{:S(2)}, u32[]{:S(2)}) async-start(f32[1,256,4,256]{3,2,0,1:T(4,128)} %copy.22), calls=%async_computation.1 | async-start | bytes 2097152 | tf_op jit(solution)/shard_map/all_to_all | solution.py:63
  94.1 55.6 %collective-permute-start = (f32[1,3,256,256]{3,2,1,0:T(8,128)}, f32[1,3,256,256]{3,2,1,0:T(8,128)S(1)}, u32[]{:S(2)}, u32[]{:S(2)}) collective-permute-start(f32[1,3,256,256]{3,2,1,0:T(8,128)} %get-tuple-element.59), channel_id=1, source_target_pairs={{0,1},{1,2},{2,3},{3,4},{4,5},{5,6},{6,7},{7,8},{8,9},{9,10},{10,1... | collective-permute-start | bytes 2359304 | tf_op jit(solution)/shard_map/ppermute | solution.py:20
  96.2 53.6 %collective-permute-start.1 = (f32[1,3,256,256]{3,2,1,0:T(8,128)S(1)}, f32[1,3,256,256]{3,2,1,0:T(8,128)S(1)}, u32[]{:S(2)}, u32[]{:S(2)}) collective-permute-start(f32[1,3,256,256]{3,2,1,0:T(8,128)S(1)} %get-tuple-element.60), channel_id=1, source_target_pairs={{1,0},{2,1},{3,2},{4,3},{5,4},{6,5},{7,6},{8,7},{9,8},{10,9},{11,1... | collective-permute-start | bytes 2359304 | tf_op jit(solution)/shard_map/ppermute | solution.py:22
  151.3 12.1 %copy-start.9 = (f32[4]{0:T(128)S(1)}, f32[4]{0:T(128)}, u32[]{:S(2)}) copy-start(f32[4]{0:T(128)} %param.18) | copy-start | bytes 52
  177.5 12.2 %copy-start.2 = (f32[1,4,256,256]{3,2,1,0:T(8,128)S(1)}, f32[1,4,256,256]{3,2,1,0:T(8,128)}, u32[]{:S(2)}) copy-start(f32[1,4,256,256]{3,2,1,0:T(8,128)} %param.14) | copy-start | bytes 3145732
  180.3 17.2 %collective-permute-start.2 = (f32[1,3,256,256]{3,2,1,0:T(8,128)}, f32[1,3,256,256]{3,2,1,0:T(8,128)}, u32[]{:S(2)}, u32[]{:S(2)}) collective-permute-start(f32[1,3,256,256]{3,2,1,0:T(8,128)} %get-tuple-element.56), channel_id=1, source_target_pairs={{63,0},{0,1},{1,2},{2,3},{3,4},{4,5},{5,6},{6,7},{7,8},{8,9},{9,10... | collective-permute-start | bytes 2359304 | tf_op jit(solution)/shard_map/ppermute | solution.py:32
  182.2 17.1 %collective-permute-start.3 = (f32[1,3,256,256]{3,2,1,0:T(8,128)}, f32[1,3,256,256]{3,2,1,0:T(8,128)}, u32[]{:S(2)}, u32[]{:S(2)}) collective-permute-start(f32[1,3,256,256]{3,2,1,0:T(8,128)} %get-tuple-element.55), channel_id=1, source_target_pairs={{1,0},{2,1},{3,2},{4,3},{5,4},{6,5},{7,6},{8,7},{9,8},{10,9},{11,1... | collective-permute-start | bytes 2359304 | tf_op jit(solution)/shard_map/ppermute | solution.py:32
  191.8 5.8 %slice-start = ((f32[1,10,256,256]{3,2,1,0:T(8,128)}), f32[1,4,256,256]{3,2,1,0:T(8,128)S(1)}, s32[]{:S(2)}) async-start(f32[1,10,256,256]{3,2,1,0:T(8,128)} %reshape.291), calls=%async_computation.5 | async-start | bytes 2097152 | tf_op jit(solution)/shard_map/slice | solution.py:83
  276.6 117.1 %all-to-all-start.3 = ((f32[1,256,4,256]{3,2,0,1:T(4,128)}), f32[1,256,4,256]{3,2,0,1:T(4,128)}, u32[]{:S(2)}, u32[]{:S(2)}) async-start(f32[1,256,4,256]{3,2,0,1:T(4,128)} %copy.27), calls=%async_computation.3 | async-start | bytes 2097152 | tf_op jit(solution)/shard_map/all_to_all | solution.py:63
  286.2 212.0 %all-reduce.2.cloned.1.call-start = ((), (), s32[]{:S(2)}) async-start(), calls=%async_computation.4 | async-start | bytes 2097152 | tf_op jit(solution)/shard_map/psum | solution.py:105
  286.4 56.5 %collective-permute-start.4 = (f32[1,3,256,256]{3,2,1,0:T(8,128)S(1)}, f32[1,3,256,256]{3,2,1,0:T(8,128)S(1)}, u32[]{:S(2)}, u32[]{:S(2)}) collective-permute-start(f32[1,3,256,256]{3,2,1,0:T(8,128)S(1)} %get-tuple-element.57), channel_id=1, source_target_pairs={{0,1},{1,2},{2,3},{3,4},{4,5},{5,6},{6,7},{7,8},{8,9},{9,10},{10,1... | collective-permute-start | bytes 2359304 | tf_op jit(solution)/shard_map/ppermute | solution.py:20
  288.4 54.4 %collective-permute-start.5 = (f32[1,3,256,256]{3,2,1,0:T(8,128)S(1)}, f32[1,3,256,256]{3,2,1,0:T(8,128)S(1)}, u32[]{:S(2)}, u32[]{:S(2)}) collective-permute-start(f32[1,3,256,256]{3,2,1,0:T(8,128)S(1)} %get-tuple-element.58), channel_id=1, source_target_pairs={{1,0},{2,1},{3,2},{4,3},{5,4},{6,5},{7,6},{8,7},{9,8},{10,9},{11,1... | collective-permute-start | bytes 2359304 | tf_op jit(solution)/shard_map/ppermute | solution.py:22
  372.5 9.5 %copy-start.8 = (f32[3]{0:T(128)S(1)}, f32[3]{0:T(128)}, u32[]{:S(2)}) copy-start(f32[3]{0:T(128)} %param.19) | copy-start | bytes 40
  372.5 10.8 %copy-start.5 = (f32[1,4,256,256]{3,2,1,0:T(8,128)S(1)}, f32[1,4,256,256]{3,2,1,0:T(8,128)}, u32[]{:S(2)}) copy-start(f32[1,4,256,256]{3,2,1,0:T(8,128)} %get-tuple-element.65) | copy-start | bytes 3145732
  372.7 17.1 %collective-permute-start.6 = (f32[1,3,256,256]{3,2,1,0:T(8,128)S(1)}, f32[1,3,256,256]{3,2,1,0:T(8,128)S(1)}, u32[]{:S(2)}, u32[]{:S(2)}) collective-permute-start(f32[1,3,256,256]{3,2,1,0:T(8,128)S(1)} %get-tuple-element.54), channel_id=1, source_target_pairs={{63,0},{0,1},{1,2},{2,3},{3,4},{4,5},{5,6},{6,7},{7,8},{8,9},{9,10... | collective-permute-start | bytes 2359304 | tf_op jit(solution)/shard_map/ppermute | solution.py:32
  374.7 16.8 %collective-permute-start.7 = (f32[1,3,256,256]{3,2,1,0:T(8,128)S(1)}, f32[1,3,256,256]{3,2,1,0:T(8,128)S(1)}, u32[]{:S(2)}, u32[]{:S(2)}) collective-permute-start(f32[1,3,256,256]{3,2,1,0:T(8,128)S(1)} %get-tuple-element.53), channel_id=1, source_target_pairs={{1,0},{2,1},{3,2},{4,3},{5,4},{6,5},{7,6},{8,7},{9,8},{10,9},{11,1... | collective-permute-start | bytes 2359304 | tf_op jit(solution)/shard_map/ppermute | solution.py:32
  393.6 5.1 %copy-start.3 = (f32[1,4,256,256]{3,2,1,0:T(8,128)S(1)}, f32[1,4,256,256]{3,2,1,0:T(8,128)}, u32[]{:S(2)}) copy-start(f32[1,4,256,256]{3,2,1,0:T(8,128)} %param.14) | copy-start | bytes 3145732
  393.6 5.1 %copy-start.4 = (f32[4,256,256]{2,1,0:T(8,128)S(1)}, f32[4,256,256]{2,1,0:T(8,128)}, u32[]{:S(2)}) copy-start(f32[4,256,256]{2,1,0:T(8,128)} %param.15) | copy-start | bytes 3145732
  393.7 5.1 %copy-start.6 = (f32[1,4,256,256]{3,2,1,0:T(8,128)S(1)}, f32[1,4,256,256]{3,2,1,0:T(8,128)}, u32[]{:S(2)}) copy-start(f32[1,4,256,256]{3,2,1,0:T(8,128)} %get-tuple-element.65) | copy-start | bytes 3145732
Sparse Core Ops, SparseCore 0:
  405.5 92.7 all-reduce.1
where the time goes:
time: 508 us; the launch traced here: 507 us
  waiting for transfers between devices  194 us (38%)
  blocking collectives  134 us (26%)
  starting transfers between devices  56.7 us (11%)
  local copies, waits for them, and re-layouts  52.9 us (10%)
  other arithmetic  33.6 us (7%)
  matrix products  22.1 us (4%)
  between operations  14.4 us (3%)
    all_to_all x2, blocking collectives, apply_hamiltonian(): lax.all_to_all(vector, 'grid', split_axis=2, concat_axis=1, tiled=True)  134 us
    ppermute x2, waiting for transfers between devices, with_halo(): lax.ppermute(tail, axis, [(i, (i + 1) % count) for i in range(count)])  93.5 us
    psum x1, waiting for transfers between devices, local(): density = lax.psum(group_density, 'orb')  92.9 us
    scatter-add x2, other arithmetic, nonlocal_term(): jnp.zeros_like(flattened).at[:, ghost_index].add(spread)  24.9 us
    gather x2, local copies, waits for them, and re-layouts, nonlocal_term(): values = flattened[:, ghost_index].reshape(orb_count, per_dev, -1)  23.6 us
    all_to_all x2, starting transfers between devices, along_z(): lax.all_to_all(turned, 'grid', split_axis=1, concat_axis=2, tiled=True)  19.4 us
    ppermute x4, starting transfers between devices, from_behind(): return lax.ppermute(block, axis, route)  18.7 us
    ppermute x2, starting transfers between devices, with_halo(): lax.ppermute(head, axis, [((i + 1) % count, i) for i in range(count)])  14.5 us
  transfers between devices with their start and end apart: 11, of which 7 were waited for; matrix products, arithmetic and copies ran while one was open for 15% of the time, Pallas kernels for 0%

commit v1 on v0

--- a/solution.py
+++ b/solution.py
@@ -102,7 +102,7 @@
         cheb_coef[0] * random_orbitals + cheb_coef[1] * first_term + cheb_coef[2] * second_term
     )
     group_density = jnp.sum(filtered * filtered, axis=0)
-    density = lax.psum(group_density, "orb")
+    density = jnp.sum(lax.all_gather(group_density, "orb"), axis=0)
     return density / (orb_count * lax.axis_size("orb"))
 
 

time: 508 us -> 592 us (1.17)
  the two profiles are of different devices: /device:TPU:4 before, /device:TPU:1 now
where the time goes in v1:
time: 592 us; the launch traced here: 591 us
  waiting for transfers between devices  280 us (47%)
  blocking collectives  138 us (23%)
  local copies, waits for them, and re-layouts  52.9 us (9%)
  starting transfers between devices  47.4 us (8%)
  other arithmetic  36.5 us (6%)
  matrix products  22.1 us (4%)
  between operations  14.4 us (2%)
    all_gather x1, waiting for transfers between devices, local(): density = jnp.sum(lax.all_gather(group_density, 'orb'), axis=0)  177 us
    all_to_all x2, blocking collectives, apply_hamiltonian(): lax.all_to_all(vector, 'grid', split_axis=2, concat_axis=1, tiled=True)  138 us
    ppermute x2, waiting for transfers between devices, with_halo(): lax.ppermute(tail, axis, [(i, (i + 1) % count) for i in range(count)])  94.7 us
    scatter-add x2, other arithmetic, nonlocal_term(): jnp.zeros_like(flattened).at[:, ghost_index].add(spread)  25 us
    gather x2, local copies, waits for them, and re-layouts, nonlocal_term(): values = flattened[:, ghost_index].reshape(orb_count, per_dev, -1)  23.6 us
    all_to_all x2, starting transfers between devices, along_z(): lax.all_to_all(turned, 'grid', split_axis=1, concat_axis=2, tiled=True)  19.8 us
    ppermute x4, starting transfers between devices, from_behind(): return lax.ppermute(block, axis, route)  16.5 us
  transfers between devices with their start and end apart: 11, of which 7 were waited for; matrix products, arithmetic and copies ran while one was open for 13% of the time, Pallas kernels for 0%

profile of v1, /device:TPU:1, one launch (start us, length us, event | category | flops | bytes accessed | tf_op | source)
XLA Modules:
  0.0 591.3 jit_solution(7609782320106821783)
XLA Ops:
  6.5 1.9 copy.20
  8.4 71.3 %all_to_all.66 = f32[1,4,256,256]{3,1,0,2:T(4,128)S(1)} all-to-all(f32[1,4,256,256]{3,1,0,2:T(4,128)S(1)} %copy.20), channel_id=1, replica_groups=mesh['orb'=8,'grid'=64] {'grid'}, dimensions={2} | all-to-all | bytes 2097152 | tf_op jit(solution)/shard_map/all_to_all | solution.py:94
  80.3 2.1 convolution_bitcast_fusion.3
  82.4 1.6 copy.22
  84.0 10.0 %all-to-all-start.1 = ((f32[1,256,4,256]{3,2,0,1:T(4,128)}), f32[1,256,4,256]{3,2,0,1:T(4,128)}, u32[]{:S(2)}, u32[]{:S(2)}) async-start(f32[1,256,4,256]{3,2,0,1:T(4,128)} %copy.22), calls=%async_computation.1 | async-start | bytes 2097152 | tf_op jit(solution)/shard_map/all_to_all | solution.py:63
  95.0 3.5 collective-permute-start
  98.6 1.9 collective-permute-start.1
  100.6 47.1 %collective-permute-done = f32[1,3,256,256]{3,2,1,0:T(8,128)S(1)} collective-permute-done((f32[1,3,256,256]{3,2,1,0:T(8,128)}, f32[1,3,256,256]{3,2,1,0:T(8,128)S(1)}, u32[]{:S(2)}, u32[]{:S(2)}) %collective-permute-start) | collective-permute-done | bytes 786464 | tf_op jit(solution)/shard_map/ppermute | solution.py:20
  147.6 2.1 collective-permute-done.1
  149.9 1.3 copy.40
  151.2 11.8 %gather_fusion = f32[2048]{0:T(1024)S(1)} fusion(f32[655360]{0:T(1024)S(1)} %bitcast.157, s32[2048]{0:T(1024)S(1)} %broadcast_clamp_fusion), kind=kCustom, calls=%fused_computation | custom fusion | bytes 24576 | tf_op jit(solution)/shard_map/gather | solution.py:73
  163.6 12.0 %scatter_custom_fusion = f32[655360]{0:T(1024)S(1)} fusion(s32[2048]{0:T(1024)S(1)} %bitcast.169, f32[2048]{0:T(1024)S(1)} %bitcast.178, f32[]{:T(128)} %constant.158.clone.1), kind=kCustom, calls=%fused_computation.14 | custom fusion | flops 2048 | bytes 2621444 | tf_op jit(solution)/shard_map/scatter-add | solution.py:78
  175.6 1.9 reshape.292
  177.5 2.8 fusion.108
  180.3 2.3 collective-permute-start.2
  182.6 6.0 %collective-permute-start.3 = (f32[1,3,256,256]{3,2,1,0:T(8,128)}, f32[1,3,256,256]{3,2,1,0:T(8,128)}, u32[]{:S(2)}, u32[]{:S(2)}) collective-permute-start(f32[1,3,256,256]{3,2,1,0:T(8,128)} %get-tuple-element.55), channel_id=1, source_target_pairs={{1,0},{2,1},{3,2},{4,3},{5,4},{6,5},{7,6},{8,7},{9,8},{10,9},{11,1... | collective-permute-start | bytes 2359304 | tf_op jit(solution)/shard_map/ppermute | solution.py:32
  188.6 2.1 convolution_bitcast_fusion.5
  190.7 1.3 copy.38
  192.0 1.5 fusion.25
  193.5 3.0 collective-permute-done.3
  196.5 1.3 fusion.24
  197.8 1.4 copy.48
  199.2 1.3 all_to_all.54
  200.6 5.2 broadcast_multiply_fusion.1
  206.4 66.5 %all_to_all.67 = f32[1,4,256,256]{3,1,0,2:T(4,128)S(1)} all-to-all(f32[1,4,256,256]{3,1,0,2:T(4,128)S(1)} %copy.25), channel_id=1, replica_groups=mesh['orb'=8,'grid'=64] {'grid'}, dimensions={2} | all-to-all | bytes 2097152 | tf_op jit(solution)/shard_map/all_to_all | solution.py:94
  273.5 2.1 convolution_bitcast_fusion
  275.6 1.7 copy.27
  277.3 9.8 %all-to-all-start.3 = ((f32[1,256,4,256]{3,2,0,1:T(4,128)}), f32[1,256,4,256]{3,2,0,1:T(4,128)}, u32[]{:S(2)}, u32[]{:S(2)}) async-start(f32[1,256,4,256]{3,2,0,1:T(4,128)} %copy.27), calls=%async_computation.3 | async-start | bytes 2097152 | tf_op jit(solution)/shard_map/all_to_all | solution.py:63
  287.3 3.5 collective-permute-start.4
  290.8 2.1 collective-permute-start.5
  293.0 47.6 %collective-permute-done.4 = f32[1,3,256,256]{3,2,1,0:T(8,128)S(1)} collective-permute-done((f32[1,3,256,256]{3,2,1,0:T(8,128)S(1)}, f32[1,3,256,256]{3,2,1,0:T(8,128)S(1)}, u32[]{:S(2)}, u32[]{:S(2)}) %collective-permute-start.4) | collective-permute-done | bytes 786464 | tf_op jit(solution)/shard_map/ppermute | solution.py:20
  340.6 2.2 collective-permute-done.5
  343.0 1.3 copy.41
  344.4 11.8 %gather_fusion.1 = f32[2048]{0:T(1024)S(1)} fusion(f32[655360]{0:T(1024)S(1)} %bitcast.156, s32[2048]{0:T(1024)S(1)} %broadcast_clamp_fusion), kind=kCustom, calls=%fused_computation.1 | custom fusion | bytes 24576 | tf_op jit(solution)/shard_map/gather | solution.py:73
  356.7 13.0 %scatter_custom_fusion.1 = f32[655360]{0:T(1024)} fusion(s32[2048]{0:T(1024)S(1)} %bitcast.170, f32[2048]{0:T(1024)S(1)} %bitcast.177, f32[]{:T(128)} %constant.158.clone.1), kind=kCustom, calls=%fused_computation.12 | custom fusion | flops 2048 | bytes 2621444 | tf_op jit(solution)/shard_map/scatter-add | solution.py:78
  369.7 2.7 reshape.297
  372.7 2.4 collective-permute-start.6
  375.1 5.8 collective-permute-start.7
  382.1 3.1 convolution_bitcast_fusion.1
  385.2 1.1 slice.193
  387.3 1.4 collective-permute-done.7
  388.7 2.2 fusion.22
  390.9 2.5 copy.46
  393.4 2.6 all_to_all.61
  396.0 6.6 %fusion.20 = f32[1,4,256,256]{3,2,1,0:T(8,128)} fusion(f32[1,4,256,256]{3,2,1,0:T(8,128)S(1)} %copy-done.3, f32[1,4,256,256]{3,2,1,0:T(8,128)} %fusion.22, f32[4,256,256]{2,1,0:T(8,128)S(1)} %copy-done.4, f32[1,4,256,256]{3,2,1,0:T(8,128)S(1)} %copy-done.6, f32[]{:T(128)} %bitcast.28, f32[]{:T(128)} %bitcast.27, f32[]{:T(128)} %bitcast, ...), kind=kOutput, calls=%fused_computation.34 | convolution fusion | flops 811270144 | bytes 7340044 | tf_op jit(solution)/shard_map/dot_general | solution.py:89
  402.5 176.8 %all-gather.2.cloned.1.call-done = f32[8,4,256,256]{3,2,1,0:T(8,128)} async-done(((f32[1,4,256,256]{3,2,1,0:T(8,128)}), f32[8,4,256,256]{3,2,1,0:T(8,128)}) %all-gather.2.cloned.1.call-update) | async-done | bytes 8388624 | tf_op jit(solution)/shard_map/all_gather | solution.py:105
  579.3 4.1 reduce_sum.8
  583.4 1.1 broadcast_multiply_fusion
  (48 shorter events, 6.3 us)
Async XLA Ops:
  6.5 156.5 %copy-start = (f32[16,4,128]{2,1,0:T(4,128)S(1)}, f32[16,4,128]{2,1,0:T(4,128)}, u32[]{:S(2)}) copy-start(f32[16,4,128]{2,1,0:T(4,128)} %param.17) | copy-start | bytes 98308
  82.3 11.6 %copy-start.1 = (f32[1,4,256,256]{3,2,1,0:T(8,128)S(1)}, f32[1,4,256,256]{3,2,1,0:T(8,128)}, u32[]{:S(2)}) copy-start(f32[1,4,256,256]{3,2,1,0:T(8,128)} %param.14) | copy-start | bytes 3145732
  84.0 16.5 %copy-start.7 = (s32[16,2,128]{2,1,0:T(2,128)S(1)}, s32[16,2,128]{2,1,0:T(2,128)}, u32[]{:S(2)}) copy-start(s32[16,2,128]{2,1,0:T(2,128)} %param.16) | copy-start | bytes 49156
  84.0 113.8 %all-to-all-start.1 = ((f32[1,256,4,256]{3,2,0,1:T(4,128)}), f32[1,256,4,256]{3,2,0,1:T(4,128)}, u32[]{:S(2)}, u32[]{:S(2)}) async-start(f32[1,256,4,256]{3,2,0,1:T(4,128)} %copy.22), calls=%async_computation.1 | async-start | bytes 2097152 | tf_op jit(solution)/shard_map/all_to_all | solution.py:63
  95.0 52.6 %collective-permute-start = (f32[1,3,256,256]{3,2,1,0:T(8,128)}, f32[1,3,256,256]{3,2,1,0:T(8,128)S(1)}, u32[]{:S(2)}, u32[]{:S(2)}) collective-permute-start(f32[1,3,256,256]{3,2,1,0:T(8,128)} %get-tuple-element.59), channel_id=1, source_target_pairs={{0,1},{1,2},{2,3},{3,4},{4,5},{5,6},{6,7},{7,8},{8,9},{9,10},{10,1... | collective-permute-start | bytes 2359304 | tf_op jit(solution)/shard_map/ppermute | solution.py:20
  98.6 51.1 %collective-permute-start.1 = (f32[1,3,256,256]{3,2,1,0:T(8,128)S(1)}, f32[1,3,256,256]{3,2,1,0:T(8,128)S(1)}, u32[]{:S(2)}, u32[]{:S(2)}) collective-permute-start(f32[1,3,256,256]{3,2,1,0:T(8,128)S(1)} %get-tuple-element.60), channel_id=1, source_target_pairs={{1,0},{2,1},{3,2},{4,3},{5,4},{6,5},{7,6},{8,7},{9,8},{10,9},{11,1... | collective-permute-start | bytes 2359304 | tf_op jit(solution)/shard_map/ppermute | solution.py:22
  151.2 12.1 %copy-start.9 = (f32[4]{0:T(128)S(1)}, f32[4]{0:T(128)}, u32[]{:S(2)}) copy-start(f32[4]{0:T(128)} %param.18) | copy-start | bytes 52
  177.5 11.1 %copy-start.2 = (f32[1,4,256,256]{3,2,1,0:T(8,128)S(1)}, f32[1,4,256,256]{3,2,1,0:T(8,128)}, u32[]{:S(2)}) copy-start(f32[1,4,256,256]{3,2,1,0:T(8,128)} %param.14) | copy-start | bytes 3145732
  180.3 11.7 %collective-permute-start.2 = (f32[1,3,256,256]{3,2,1,0:T(8,128)}, f32[1,3,256,256]{3,2,1,0:T(8,128)}, u32[]{:S(2)}, u32[]{:S(2)}) collective-permute-start(f32[1,3,256,256]{3,2,1,0:T(8,128)} %get-tuple-element.56), channel_id=1, source_target_pairs={{63,0},{0,1},{1,2},{2,3},{3,4},{4,5},{5,6},{6,7},{7,8},{8,9},{9,10... | collective-permute-start | bytes 2359304 | tf_op jit(solution)/shard_map/ppermute | solution.py:32
  182.6 13.9 %collective-permute-start.3 = (f32[1,3,256,256]{3,2,1,0:T(8,128)}, f32[1,3,256,256]{3,2,1,0:T(8,128)}, u32[]{:S(2)}, u32[]{:S(2)}) collective-permute-start(f32[1,3,256,256]{3,2,1,0:T(8,128)} %get-tuple-element.55), channel_id=1, source_target_pairs={{1,0},{2,1},{3,2},{4,3},{5,4},{6,5},{7,6},{8,7},{9,8},{10,9},{11,1... | collective-permute-start | bytes 2359304 | tf_op jit(solution)/shard_map/ppermute | solution.py:32
  190.7 1.3 slice-start
  277.3 113.6 %all-to-all-start.3 = ((f32[1,256,4,256]{3,2,0,1:T(4,128)}), f32[1,256,4,256]{3,2,0,1:T(4,128)}, u32[]{:S(2)}, u32[]{:S(2)}) async-start(f32[1,256,4,256]{3,2,0,1:T(4,128)} %copy.27), calls=%async_computation.3 | async-start | bytes 2097152 | tf_op jit(solution)/shard_map/all_to_all | solution.py:63
  287.1 292.2 %all-gather.2.cloned.1.call-start = ((), (), s32[]{:S(2)}) async-start(), calls=%async_computation.4 | async-start | bytes 9437184 | tf_op jit(solution)/shard_map/all_gather | solution.py:105
  287.3 53.3 %collective-permute-start.4 = (f32[1,3,256,256]{3,2,1,0:T(8,128)S(1)}, f32[1,3,256,256]{3,2,1,0:T(8,128)S(1)}, u32[]{:S(2)}, u32[]{:S(2)}) collective-permute-start(f32[1,3,256,256]{3,2,1,0:T(8,128)S(1)} %get-tuple-element.57), channel_id=1, source_target_pairs={{0,1},{1,2},{2,3},{3,4},{4,5},{5,6},{6,7},{7,8},{8,9},{9,10},{10,1... | collective-permute-start | bytes 2359304 | tf_op jit(solution)/shard_map/ppermute | solution.py:20
  290.8 52.0 %collective-permute-start.5 = (f32[1,3,256,256]{3,2,1,0:T(8,128)S(1)}, f32[1,3,256,256]{3,2,1,0:T(8,128)S(1)}, u32[]{:S(2)}, u32[]{:S(2)}) collective-permute-start(f32[1,3,256,256]{3,2,1,0:T(8,128)S(1)} %get-tuple-element.58), channel_id=1, source_target_pairs={{1,0},{2,1},{3,2},{4,3},{5,4},{6,5},{7,6},{8,7},{9,8},{10,9},{11,1... | collective-permute-start | bytes 2359304 | tf_op jit(solution)/shard_map/ppermute | solution.py:22
  372.4 8.4 %copy-start.8 = (f32[3]{0:T(128)S(1)}, f32[3]{0:T(128)}, u32[]{:S(2)}) copy-start(f32[3]{0:T(128)} %param.19) | copy-start | bytes 40
  372.5 9.7 %copy-start.5 = (f32[1,4,256,256]{3,2,1,0:T(8,128)S(1)}, f32[1,4,256,256]{3,2,1,0:T(8,128)}, u32[]{:S(2)}) copy-start(f32[1,4,256,256]{3,2,1,0:T(8,128)} %get-tuple-element.65) | copy-start | bytes 3145732
  372.7 13.7 %collective-permute-start.6 = (f32[1,3,256,256]{3,2,1,0:T(8,128)S(1)}, f32[1,3,256,256]{3,2,1,0:T(8,128)S(1)}, u32[]{:S(2)}, u32[]{:S(2)}) collective-permute-start(f32[1,3,256,256]{3,2,1,0:T(8,128)S(1)} %get-tuple-element.54), channel_id=1, source_target_pairs={{63,0},{0,1},{1,2},{2,3},{3,4},{4,5},{5,6},{6,7},{7,8},{8,9},{9,10... | collective-permute-start | bytes 2359304 | tf_op jit(solution)/shard_map/ppermute | solution.py:32
  375.1 13.6 %collective-permute-start.7 = (f32[1,3,256,256]{3,2,1,0:T(8,128)S(1)}, f32[1,3,256,256]{3,2,1,0:T(8,128)S(1)}, u32[]{:S(2)}, u32[]{:S(2)}) collective-permute-start(f32[1,3,256,256]{3,2,1,0:T(8,128)S(1)} %get-tuple-element.53), channel_id=1, source_target_pairs={{1,0},{2,1},{3,2},{4,3},{5,4},{6,5},{7,6},{8,7},{9,8},{10,9},{11,1... | collective-permute-start | bytes 2359304 | tf_op jit(solution)/shard_map/ppermute | solution.py:32
  390.8 5.1 copy-start.3
  390.8 5.1 copy-start.4
  390.8 5.1 copy-start.6
Sparse Core Ops, SparseCore 0:
  402.7 176.5 all-gather.1
